TPU v7x, 128 devices: a whole 4x4x4 slice. The times are simulated.
128 devices in a mesh: dp: 32 (over z, y, core), ctx: 4 (over x).
Axes of the slice: x: 4, y: 4, z: 4, core: 2. Of those that a mesh axis runs over, the one named last changes fastest.
Arguments:
- q_rows: bfloat16 [16384, 8192], P(('dp', 'ctx')), may hold values from -6 to 6
- k_rows: bfloat16 [16384, 8192], P(('dp', 'ctx')), may hold values from -6 to 6
- v_rows: bfloat16 [16384, 8192], P(('dp', 'ctx')), may hold values from -6 to 6
- out_grad: bfloat16 [16384, 8192], P(('dp', 'ctx')), may hold values from -24 to 24
- filters: float32 [512, 128], replicated, may hold values from -0.5 to 0.5
- skip_gain: float32 [8192], replicated, may hold values from -4 to 4
- genome_len: int32 [32, 3], P('dp'), may hold values from 1 to 256, 512 in all within a row
- plan_offset: int32 [128, 128, 1], P(None, ('dp', 'ctx')), may hold values from 0 to 127, as said below
Outputs:
- mixer_out: bfloat16 [16384, 8192], P(('dp', 'ctx'))
- q_grad: bfloat16 [16384, 8192], P(('dp', 'ctx'))
- k_grad: bfloat16 [16384, 8192], P(('dp', 'ctx'))
- v_grad: bfloat16 [16384, 8192], P(('dp', 'ctx'))
- filter_grad: float32 [512, 128], P(('dp', 'ctx'))
- skip_grad: float32 [8192], P(('dp', 'ctx'))
Inputs may be any that keep to these rules, and one draw needn't show every extreme that they name: For every member b, the values plan_offset[a, b, c] over all loaders a and slots c are each of 0 to 127 exactly once, and each loader's slots for b are one run of 1 row, plan_offset[a, b, c] = plan_offset[a, b, 0] + c, starting at a multiple of 1.
All inputs are finite; a program needn't handle non-finite values.
Results may differ from a plain program's by a relative error of at most 0.0056.
Values may be sent and summed in bfloat16 or wider, within the bound.
A program may use at most 320 MiB of HBM per device.

v0:
```python
import math

import jax
import jax.numpy as jnp
from jax import lax
from jax.sharding import PartitionSpec as P


def shifted(block, axis, distance):
    devices = range(lax.axis_size(axis))
    route = [(i - distance, i) for i in devices if i - distance in devices]
    return lax.ppermute(block, axis, route)


def toeplitz(edge):
    group_here, span = edge.shape
    tap_count = (span - 1) // 2
    tiled = jnp.tile(edge, (1, tap_count))
    return tiled[:, : 2 * tap_count * tap_count].reshape(group_here, tap_count, 2 * tap_count)


def windows(extended, tap_count):
    blocks = extended.reshape(extended.shape[0] // tap_count, tap_count, extended.shape[1])
    return jnp.concatenate([blocks[:-1], blocks[1:]], axis=1)


def diagonal_sums(square):
    group_here, tap_count, _ = square.shape
    flat = square.reshape(group_here, tap_count * tap_count)[:, : tap_count * tap_count - 1]
    return jnp.sum(flat.reshape(group_here, tap_count - 1, tap_count + 1), axis=1)


def body(q_rows, k_rows, v_rows, out_grad, filters, skip_gain, genome_len, plan_offset):
    row_count, chan_count = q_rows.shape
    dp_size = lax.axis_size("dp")
    ctx_size = lax.axis_size("ctx")
    members = dp_size * ctx_size
    per_member = row_count // members
    group_count, tap_count = filters.shape
    per_group = chan_count // group_count
    block_count = row_count // tap_count
    step_groups = min(group_count, 128)
    step_chans = step_groups * per_group
    piece_count = genome_len.shape[1]
    mixed = (k_rows.astype(jnp.float32) * v_rows.astype(jnp.float32)).astype(jnp.bfloat16)
    member_query, member_mixed = (
        lax.all_to_all(
            q_rows.reshape(members, per_member, chan_count),
            ("dp", "ctx"),
            split_axis=0,
            concat_axis=0,
            tiled=True,
        ),
        lax.all_to_all(
            mixed.reshape(members, per_member, chan_count),
            ("dp", "ctx"),
            split_axis=0,
            concat_axis=0,
            tiled=True,
        ),
    )
    offsets = plan_offset.reshape(-1)
    inverse = (
        jnp.zeros((row_count,), jnp.int32).at[offsets].set(jnp.arange(row_count, dtype=jnp.int32))
    )
    planned_query = member_query.reshape(row_count, chan_count)[inverse]
    planned_mixed = member_mixed.reshape(row_count, chan_count)[inverse]
    earlier = shifted(planned_mixed, "ctx", 1)
    mixed_windows = windows(jnp.concatenate([earlier, planned_mixed], axis=0), tap_count)
    ends = jnp.cumsum(genome_len.reshape(-1))
    first_row = lax.axis_index("ctx") * row_count
    position = first_row - tap_count + jnp.arange(row_count + 2 * tap_count, dtype=jnp.int32)
    inside = (position >= 0) & (position < row_count * ctx_size)
    segment = jnp.sum((position[:, None] >= ends[None, :]).astype(jnp.int32), axis=1)
    segment = jnp.where(inside, segment, -1)
    seg_blocks = segment.reshape(block_count + 2, tap_count)
    own_seg = seg_blocks[1 : block_count + 1]
    back_seg = jnp.concatenate([seg_blocks[:block_count], own_seg], axis=1)
    ahead_seg = jnp.concatenate([own_seg, seg_blocks[2:]], axis=1)
    piece_ids = jnp.arange(piece_count, dtype=jnp.int32)
    own_hit = own_seg[None] == piece_ids[:, None, None]
    back_hit = back_seg[None] == piece_ids[:, None, None]
    ahead_hit = ahead_seg[None] == piece_ids[:, None, None]
    taps_b = filters.astype(jnp.bfloat16)
    edge_back = jnp.concatenate(
        [
            jnp.zeros((group_count, 1), jnp.bfloat16),
            taps_b[:, ::-1],
            jnp.zeros((group_count, tap_count), jnp.bfloat16),
        ],
        axis=1,
    )
    firsts = list(range(0, group_count, step_groups))
    matrices = [toeplitz(edge_back[first : first + step_groups]) for first in firsts]
    zero_b = jnp.zeros((), jnp.bfloat16)

    def split_pieces(window_rows, hit, first):
        piece = window_rows[:, :, first * per_group : first * per_group + step_chans]
        stacked = jnp.where(hit[:, :, :, None], piece[None], zero_b)
        return stacked.reshape(
            piece_count, block_count, window_rows.shape[1], step_groups, per_group
        )

    def keep_own(result):
        kept = jnp.sum(jnp.where(own_hit[:, :, :, None, None], result, 0.0), axis=0)
        return kept.reshape(row_count, step_chans)

    mixed_pieces = [split_pieces(mixed_windows, back_hit, first) for first in firsts]
    filtered = jnp.concatenate(
        [
            keep_own(
                jnp.einsum("gim,sbmgc->sbigc", matrix, pieces, preferred_element_type=jnp.float32)
            )
            for matrix, pieces in zip(matrices, mixed_pieces)
        ],
        axis=1,
    )
    mixed_f = planned_mixed.astype(jnp.float32)
    query_f = planned_query.astype(jnp.float32)
    grad_f = out_grad.astype(jnp.float32)
    gated = filtered + skip_gain[None, :] * mixed_f
    mixer_out = (query_f * gated).astype(jnp.bfloat16)
    query_grad = (grad_f * gated).astype(jnp.bfloat16)
    inner = grad_f * query_f
    inner_b = inner.astype(jnp.bfloat16)
    later = shifted(inner_b, "ctx", -1)
    grad_windows = windows(jnp.concatenate([inner_b, later], axis=0), tap_count)
    back_parts = []
    filter_parts = []
    for matrix, pieces, first in zip(matrices, mixed_pieces, firsts):
        grad_pieces = split_pieces(grad_windows, ahead_hit, first)
        halves = grad_pieces.reshape(
            piece_count, block_count, 2, tap_count, step_groups, per_group
        )[:, :, ::-1]
        folded = matrix.reshape(step_groups, tap_count, 2, tap_count)
        back_parts.append(
            keep_own(
                jnp.einsum("gkhi,sbhkgc->sbigc", folded, halves, preferred_element_type=jnp.float32)
            )
        )
        own_grads = grad_pieces[:, :, :tap_count]
        before = jnp.einsum(
            "sbigc,sbmgc->gim",
            own_grads,
            pieces[:, :, :tap_count],
            preferred_element_type=jnp.float32,
        )
        same = jnp.einsum(
            "sbigc,sbmgc->gim",
            own_grads,
            pieces[:, :, tap_count:],
            preferred_element_type=jnp.float32,
        )
        row_idx = jnp.arange(tap_count, dtype=jnp.int32)[:, None]
        col_idx = jnp.arange(tap_count, dtype=jnp.int32)[None, :]
        lower = jnp.where((col_idx <= row_idx)[None], same, 0.0)
        upper = jnp.where((col_idx > row_idx)[None], before, 0.0)
        lower_sums = diagonal_sums(lower)
        upper_sums = diagonal_sums(upper)
        lag_zero = lower_sums[:, :1] + lower[:, tap_count - 1, tap_count - 1 :]
        from_lower = jnp.concatenate([lag_zero, lower_sums[:, 2:][:, ::-1]], axis=1)
        from_upper = jnp.concatenate(
            [jnp.zeros((step_groups, 1), jnp.float32), upper_sums[:, 1:tap_count][:, ::-1]], axis=1
        )
        filter_parts.append(from_lower + from_upper)
    back_conv = jnp.concatenate(back_parts, axis=1)
    mixed_grad = (back_conv + skip_gain[None, :] * inner).astype(jnp.bfloat16)
    filter_local = jnp.concatenate(filter_parts, axis=0)
    skip_local = jnp.sum(inner * mixed_f, axis=0)
    filter_sum, skip_sum = (
        lax.psum_scatter(filter_local, ("dp", "ctx"), scatter_dimension=0, tiled=True),
        lax.psum_scatter(skip_local, ("dp", "ctx"), scatter_dimension=0, tiled=True),
    )
    total_tokens = row_count * members
    filter_grad = filter_sum / math.sqrt(total_tokens * per_group)
    skip_grad = skip_sum / math.sqrt(total_tokens)
    back_query = query_grad[offsets]
    back_mixed = mixed_grad[offsets]
    loader_query, loader_mixed = (
        lax.all_to_all(
            back_query.reshape(members, per_member, chan_count),
            ("dp", "ctx"),
            split_axis=0,
            concat_axis=0,
            tiled=True,
        ),
        lax.all_to_all(
            back_mixed.reshape(members, per_member, chan_count),
            ("dp", "ctx"),
            split_axis=0,
            concat_axis=0,
            tiled=True,
        ),
    )
    q_grad = loader_query.reshape(row_count, chan_count)
    loader_grad = loader_mixed.reshape(row_count, chan_count).astype(jnp.float32)
    k_grad = (loader_grad * v_rows.astype(jnp.float32)).astype(jnp.bfloat16)
    v_grad = (loader_grad * k_rows.astype(jnp.float32)).astype(jnp.bfloat16)
    return (mixer_out, q_grad, k_grad, v_grad, filter_grad, skip_grad)


def solution(mesh):
    placed = (
        P(("dp", "ctx"), None),
        P(("dp", "ctx"), None),
        P(("dp", "ctx"), None),
        P(("dp", "ctx"), None),
        P(),
        P(),
        P("dp", None),
        P(None, ("dp", "ctx"), None),
    )
    return jax.shard_map(
        body,
        mesh=mesh,
        in_specs=placed,
        out_specs=(
            P(("dp", "ctx"), None),
            P(("dp", "ctx"), None),
            P(("dp", "ctx"), None),
            P(("dp", "ctx"), None),
            P(("dp", "ctx"), None),
            P(("dp", "ctx")),
        ),
        check_vma=False,
    )
```

profile of v0, /device:TPU:1, one launch (start us, length us, event | category | flops | bytes accessed | tf_op | source)
XLA Modules:
  0.0 911.5 jit_solution(13139006991609241286)
XLA Ops:
  14.3 11.5 %all-to-all-start = ((bf16[128,2,4096]{2,1,0:T(2,128)(2,1)}), bf16[128,2,4096]{2,1,0:T(2,128)(2,1)S(1)}, u32[]{:S(2)}, u32[]{:S(2)}) async-start(bf16[128,2,4096]{2,1,0:T(2,128)(2,1)} %reshape.629), calls=%async_computation | async-start | bytes 4194304 | tf_op jit(solution)/shard_map/all_to_all | solution.py:47
  38.8 17.8 %all-to-all-done = bf16[128,2,4096]{2,1,0:T(2,128)(2,1)S(1)} async-done(((bf16[128,2,4096]{2,1,0:T(2,128)(2,1)}), bf16[128,2,4096]{2,1,0:T(2,128)(2,1)S(1)}, u32[]{:S(2)}, u32[]{:S(2)}) %all-to-all-start) | async-done | bytes 2097184 | tf_op jit(solution)/shard_map/all_to_all | solution.py:47
  74.4 17.7 %all-to-all-done.1 = bf16[128,2,4096]{2,1,0:T(2,128)(2,1)} async-done(((bf16[128,2,4096]{2,1,0:T(2,128)(2,1)}), bf16[128,2,4096]{2,1,0:T(2,128)(2,1)}, u32[]{:S(2)}, u32[]{:S(2)}) %all-to-all-start.1) | async-done | bytes 2097184 | tf_op jit(solution)/shard_map/all_to_all | solution.py:54
  92.2 13.8 %reshape.632 = bf16[128,1,8192]{2,1,0:T(2,128)(2,1)} reshape(bf16[128,2,4096]{2,1,0:T(2,128)(2,1)} %all-to-all-done.1) | data formatting | bytes 4194304
  136.3 12.9 %tile.19 = bf16[128,32896]{0,1:T(8,128)(2,1)} reshape(bf16[128,128,257]{0,2,1:T(8,128)(2,1)} %tile.18) | data formatting | bytes 16842752 | tf_op jit(solution)/shard_map/tile | solution.py:18
  156.3 12.8 %copy.225 = bf16[128,128,256,1]{2,1,3,0:T(8,128)(2,1)} copy(bf16[128,128,256,1]{0,2,1,3:T(8,128)(2,1)} %bitcast.291) | data formatting | bytes 16777216 | tf_op jit(solution)/shard_map/reshape | solution.py:19
  169.0 12.5 %copy.230 = bf16[128,128,2,128,1]{3,1,2,4,0:T(8,128)(2,1)} copy(bf16[128,128,2,128,1]{0,3,2,1,4:T(8,128)(2,1)} %bitcast.292) | data formatting | bytes 16777216 | tf_op jit(solution)/shard_map/reshape;reshape | solution.py:135
  185.9 12.9 %tile.41 = bf16[128,32896]{0,1:T(8,128)(2,1)} reshape(bf16[128,128,257]{0,2,1:T(8,128)(2,1)} %tile.40) | data formatting | bytes 16842752 | tf_op jit(solution)/shard_map/tile | solution.py:18
  205.9 12.5 %copy.226 = bf16[128,128,256,1]{2,1,3,0:T(8,128)(2,1)} copy(bf16[128,128,256,1]{0,2,1,3:T(8,128)(2,1)} %bitcast.293) | data formatting | bytes 16777216 | tf_op jit(solution)/shard_map/reshape | solution.py:19
  218.4 12.4 %copy.232 = bf16[128,128,2,128,1]{3,1,2,4,0:T(8,128)(2,1)} copy(bf16[128,128,2,128,1]{0,3,2,1,4:T(8,128)(2,1)} %bitcast.294) | data formatting | bytes 16777216 | tf_op jit(solution)/shard_map/reshape;reshape | solution.py:135
  235.2 12.9 %tile.43 = bf16[128,32896]{0,1:T(8,128)(2,1)} reshape(bf16[128,128,257]{0,2,1:T(8,128)(2,1)} %tile.42) | data formatting | bytes 16842752 | tf_op jit(solution)/shard_map/tile | solution.py:18
  255.2 12.3 %copy.227 = bf16[128,128,256,1]{2,1,3,0:T(8,128)(2,1)} copy(bf16[128,128,256,1]{0,2,1,3:T(8,128)(2,1)} %bitcast.295) | data formatting | bytes 16777216 | tf_op jit(solution)/shard_map/reshape | solution.py:19
  267.5 12.4 %copy.234 = bf16[128,128,2,128,1]{3,1,2,4,0:T(8,128)(2,1)} copy(bf16[128,128,2,128,1]{0,3,2,1,4:T(8,128)(2,1)} %bitcast.296) | data formatting | bytes 16777216 | tf_op jit(solution)/shard_map/reshape;reshape | solution.py:135
  284.4 12.9 %tile.17 = bf16[128,32896]{0,1:T(8,128)(2,1)} reshape(bf16[128,128,257]{0,2,1:T(8,128)(2,1)} %tile.16) | data formatting | bytes 16842752 | tf_op jit(solution)/shard_map/tile | solution.py:18
  304.3 12.3 %copy.224 = bf16[128,128,256,1]{2,1,3,0:T(8,128)(2,1)} copy(bf16[128,128,256,1]{0,2,1,3:T(8,128)(2,1)} %bitcast.297) | data formatting | bytes 16777216 | tf_op jit(solution)/shard_map/reshape | solution.py:19
  316.6 12.6 %copy.228 = bf16[128,128,2,128,1]{3,1,2,4,0:T(8,128)(2,1)} copy(bf16[128,128,2,128,1]{0,3,2,1,4:T(8,128)(2,1)} %bitcast.298) | data formatting | bytes 16777216 | tf_op jit(solution)/shard_map/reshape;reshape | solution.py:135
  523.5 9.4 %copy.264 = f32[128,128,128]{0,2,1:T(8,128)} copy(f32[128,128,128]{2,1,0:T(8,128)} %bitcast_select_fusion.7) | data formatting | bytes 16777216 | tf_op jit(solution)/shard_map/reshape | solution.py:29
  546.0 9.4 %copy.265 = f32[128,128,128]{0,2,1:T(8,128)} copy(f32[128,128,128]{2,1,0:T(8,128)} %bitcast_select_fusion.6) | data formatting | bytes 16777216 | tf_op jit(solution)/shard_map/reshape | solution.py:29
  568.5 9.4 %copy.266 = f32[128,128,128]{0,2,1:T(8,128)} copy(f32[128,128,128]{2,1,0:T(8,128)} %bitcast_select_fusion.5) | data formatting | bytes 16777216 | tf_op jit(solution)/shard_map/reshape | solution.py:29
  613.5 9.4 %copy.268 = f32[128,128,128]{0,2,1:T(8,128)} copy(f32[128,128,128]{2,1,0:T(8,128)} %bitcast_select_fusion.3) | data formatting | bytes 16777216 | tf_op jit(solution)/shard_map/reshape | solution.py:29
  658.4 9.4 %copy.270 = f32[128,128,128]{0,2,1:T(8,128)} copy(f32[128,128,128]{2,1,0:T(8,128)} %bitcast_select_fusion.1) | data formatting | bytes 16777216 | tf_op jit(solution)/shard_map/reshape | solution.py:29
  725.8 67.7 %all-reduce.5 = f32[8192]{0:T(1024)S(1)} all-reduce(f32[8192]{0:T(1024)S(1)} %get-tuple-element.38), channel_id=3, replica_groups=mesh['dp'=32,'ctx'=4] {'dp','ctx'}, use_global_device_ids=true, to_apply=%region_21.22.clone | all-reduce | flops 8192 | bytes 65536
  799.3 68.2 %all-reduce.8.cloned.1.call-done = f32[512,128]{0,1:T(8,128)} async-done(((f32[512,128]{0,1:T(8,128)}), f32[512,128]{0,1:T(8,128)}) %all-reduce.8.cloned.1.call-update) | async-done | bytes 262160
  869.1 13.8 %reshape.636 = bf16[128,1,8192]{2,1,0:T(2,128)(2,1)} reshape(bf16[128,2,4096]{2,1,0:T(2,128)(2,1)} %all-to-all-done.3) | data formatting | bytes 4194304
  (206 shorter events, 487.8 us)
Async XLA Ops:
  14.3 42.3 %all-to-all-start = ((bf16[128,2,4096]{2,1,0:T(2,128)(2,1)}), bf16[128,2,4096]{2,1,0:T(2,128)(2,1)S(1)}, u32[]{:S(2)}, u32[]{:S(2)}) async-start(bf16[128,2,4096]{2,1,0:T(2,128)(2,1)} %reshape.629), calls=%async_computation | async-start | bytes 4194304 | tf_op jit(solution)/shard_map/all_to_all | solution.py:47
  38.8 22.8 %copy-start.15 = (s32[1,3]{1,0:T(1,128)S(1)}, s32[1,3]{1,0:T(1,128)}, u32[]{:S(2)}) copy-start(s32[1,3]{1,0:T(1,128)} %param.14) | copy-start | bytes 40
  38.8 23.0 %copy-start.16 = (s32[128,1,1]{0,2,1:T(1,128)S(1)}, s32[128,1,1]{0,2,1:T(1,128)}, u32[]{:S(2)}) copy-start(s32[128,1,1]{0,2,1:T(1,128)} %param.15) | copy-start | bytes 1540
  56.7 35.5 %all-to-all-start.1 = ((bf16[128,2,4096]{2,1,0:T(2,128)(2,1)}), bf16[128,2,4096]{2,1,0:T(2,128)(2,1)}, u32[]{:S(2)}, u32[]{:S(2)}) async-start(bf16[128,2,4096]{2,1,0:T(2,128)(2,1)} %reshape.631), calls=%async_computation.1 | async-start | bytes 4194304 | tf_op jit(solution)/shard_map/all_to_all | solution.py:54
  115.0 10.8 %copy-start = (bf16[128,8192]{1,0:T(8,128)(2,1)S(1)}, bf16[128,8192]{1,0:T(8,128)(2,1)}, u32[]{:S(2)}) copy-start(bf16[128,8192]{1,0:T(8,128)(2,1)} %gather_fusion) | copy-start | bytes 6291460
  122.1 8.6 copy-start.13
  122.1 207.2 %collective-permute-start = (bf16[128,8192]{1,0:T(8,128)(2,1)}, bf16[128,8192]{1,0:T(8,128)(2,1)}, u32[]{:S(2)}, u32[]{:S(2)}) collective-permute-start(bf16[128,8192]{1,0:T(8,128)(2,1)} %gather_fusion.1), channel_id=1, source_target_pairs={{0,1},{1,2},{2,3},{4,5},{5,6},{6,7},{8,9},{9,10},{10,11},{12,13},{... | collective-permute-start | bytes 6291464 | tf_op jit(solution)/shard_map/ppermute | solution.py:12
  129.2 208.8 %collective-permute-start.1 = (bf16[128,8192]{1,0:T(8,128)(2,1)}, bf16[128,8192]{1,0:T(8,128)(2,1)}, u32[]{:S(2)}, u32[]{:S(2)}) collective-permute-start(bf16[128,8192]{1,0:T(8,128)(2,1)} %fusion.8), channel_id=1, source_target_pairs={{1,0},{2,1},{3,2},{5,4},{6,5},{7,6},{9,8},{10,9},{11,10},{13,12},{... | collective-permute-start | bytes 6291464 | tf_op jit(solution)/shard_map/ppermute | solution.py:12
  316.6 12.7 %copy-start.1 = (bf16[128,8192]{1,0:T(8,128)(2,1)S(1)}, bf16[128,8192]{1,0:T(8,128)(2,1)}, u32[]{:S(2)}) copy-start(bf16[128,8192]{1,0:T(8,128)(2,1)} %gather_fusion.1) | copy-start | bytes 6291460
  332.2 4.4 copy-start.8
  333.8 14.4 %copy-start.2 = (bf16[1,256,2048]{1,2,0:T(8,128)(2,1)}, bf16[1,256,2048]{1,2,0:T(8,128)(2,1)S(1)}, u32[]{:S(2)}) copy-start(bf16[1,256,2048]{1,2,0:T(8,128)(2,1)S(1)} %copy.176) | copy-start | bytes 3145732
  336.6 11.6 %copy-start.3 = (bf16[1,256,2048]{1,2,0:T(8,128)(2,1)}, bf16[1,256,2048]{1,2,0:T(8,128)(2,1)S(1)}, u32[]{:S(2)}) copy-start(bf16[1,256,2048]{1,2,0:T(8,128)(2,1)S(1)} %copy.185) | copy-start | bytes 3145732
  348.2 4.6 copy-start.12
  366.3 4.6 copy-start.7
  371.9 6.1 copy-start.10
  378.0 4.5 copy-start.6
  383.3 1.4 copy-start.5
  384.2 1.3 copy-start.4
  475.5 7.6 copy-start.14
  506.3 6.5 copy-start.11
  506.3 287.8 %all-to-all-start.3 = ((bf16[128,2,4096]{2,1,0:T(2,128)(2,1)}), bf16[128,2,4096]{2,1,0:T(2,128)(2,1)}, u32[]{:S(2)}, u32[]{:S(2)}) async-start(bf16[128,2,4096]{2,1,0:T(2,128)(2,1)} %reshape.635), calls=%async_computation.3 | async-start | bytes 4194304 | tf_op jit(solution)/shard_map/all_to_all | solution.py:187
  512.8 354.7 %all-reduce.8.cloned.1.call-start = ((), (), s32[]{:S(2)}) async-start(), calls=%async_computation.4 | async-start | bytes 524288
  512.8 6.1 copy-start.9
  794.1 97.7 %all-to-all-start.2 = ((bf16[128,2,4096]{2,1,0:T(2,128)(2,1)}), bf16[128,2,4096]{2,1,0:T(2,128)(2,1)S(1)}, u32[]{:S(2)}, u32[]{:S(2)}) async-start(bf16[128,2,4096]{2,1,0:T(2,128)(2,1)} %reshape.633), calls=%async_computation.2 | async-start | bytes 4194304 | tf_op jit(solution)/shard_map/all_to_all | solution.py:180
Sparse Core Ops, SparseCore 0:
  716.1 151.3 all-reduce.7
where the time goes:
time: 925 us; the launch traced here: 911 us
  local copies, waits for them, and re-layouts  503 us (54%)
  waiting for transfers between devices  104 us (11%)
  matrix products  97.6 us (11%)
  other arithmetic  91.2 us (10%)
  blocking collectives  67.7 us (7%)
  starting transfers between devices  33.3 us (4%)
  between operations  14.9 us (2%)
    reshape x8, local copies, waits for them, and re-layouts, diagonal_sums(): square.reshape(group_here, tap_count * tap_count)  74.8 us
    unnamed x46, local copies, waits for them, and re-layouts  73.3 us
    reshape x8, local copies, waits for them, and re-layouts, diagonal_sums(): flat.reshape(group_here, tap_count - 1, tap_count + 1)  73.2 us
    another operation x8, local copies, waits for them, and re-layouts, toeplitz(): tiled = jnp.tile(edge, (1, tap_count))  69.4 us
    unnamed x2, waiting for transfers between devices  68.2 us
    unnamed x1, blocking collectives  67.7 us
    another operation x4, local copies, waits for them, and re-layouts, body(): folded = matrix.reshape(step_groups, tap_count, 2, tap_count)  49.9 us
    reshape x4, local copies, waits for them, and re-layouts, toeplitz(): tiled[:, :2 * tap_count * tap_count]  49.8 us
  transfers between devices with their start and end apart: 7, of which 3 were waited for; matrix products, arithmetic and copies ran while one was open for 52% of the time, Pallas kernels for 0%

commit v1 on v0

v1 whole, which is shorter than its diff:
```python
import functools
import math

import jax
import jax.numpy as jnp
from jax import lax
from jax.experimental import pallas as pl
from jax.experimental.pallas import tpu as pltpu
from jax.sharding import PartitionSpec as P

BF = jnp.bfloat16
F32 = jnp.float32
T = 128
STEP = 16
NC = 2


def dot(a, b, dims=((1,), (0,))):
    return lax.dot_general(a, b, (dims, ((), ())), preferred_element_type=F32)


def lanes(r):
    return slice(r * T, (r + 1) * T)


def prep_kernel(q_ref, k_ref, v_ref, out_ref, sc):
    for r in range(STEP):
        sc[:, r, :] = q_ref[:, lanes(r)].astype(F32)
    out_ref[:, 0] = sc[...].astype(BF)
    for r in range(STEP):
        sc[:, r, :] = k_ref[:, lanes(r)].astype(F32) * v_ref[:, lanes(r)].astype(F32)
    out_ref[:, 1] = sc[...].astype(BF)


def prep(q, k, v, first, blocks):
    wide = pl.BlockSpec((T, STEP * T), lambda i: (0, first // STEP + i))
    return pl.pallas_call(
        prep_kernel,
        grid=(blocks // STEP,),
        in_specs=[wide] * 3,
        out_specs=pl.BlockSpec((T, 2, STEP, T), lambda i: (0, 0, i, 0)),
        out_shape=jax.ShapeDtypeStruct((T, 2, blocks, T), BF),
        scratch_shapes=[pltpu.VMEM((T, STEP, T), F32)],
        compiler_params=pltpu.CompilerParams(vmem_limit_bytes=40 * 2**20),
        name="prep",
    )(q, k, v)


def plan_kernel(got_ref, grad_ref, off_ref, q_ref, u_ref, inner_ref, sc):
    rows = lax.broadcasted_iota(jnp.int32, (T, T), 0)
    place = (rows == off_ref[...]).astype(BF)
    sc[...] = got_ref[...].astype(F32)
    for r in range(STEP):
        both = jnp.concatenate([sc[:, 0, r, :], sc[:, 1, r, :]], axis=1).astype(BF)
        planned = dot(place, both)
        q_ref[:, lanes(r)] = planned[:, :T].astype(BF)
        u_ref[:, lanes(r)] = planned[:, T:].astype(BF)
        inner_ref[:, lanes(r)] = (grad_ref[:, lanes(r)].astype(F32) * planned[:, :T]).astype(BF)


def plan(got, grad, off_row, first):
    blocks = got.shape[2]
    wide = pl.BlockSpec((T, STEP * T), lambda i: (0, i))
    there = pl.BlockSpec((T, STEP * T), lambda i: (0, first // STEP + i))
    flat = jax.ShapeDtypeStruct((T, blocks * T), BF)
    return pl.pallas_call(
        plan_kernel,
        grid=(blocks // STEP,),
        in_specs=[
            pl.BlockSpec((T, 2, STEP, T), lambda i: (0, 0, i, 0)),
            there,
            pl.BlockSpec((1, T), lambda i: (0, 0)),
        ],
        out_specs=[wide] * 3,
        out_shape=[flat] * 3,
        scratch_shapes=[pltpu.VMEM((T, 2, STEP, T), F32)],
        compiler_params=pltpu.CompilerParams(vmem_limit_bytes=40 * 2**20),
        name="plan",
    )(got, grad, off_row)


def turned(row):
    full = jnp.broadcast_to(row, (T, T))
    return pltpu.roll(full, 0, 1, stride=1, stride_axis=0)


def conv_block(u2, i2, taps, rtaps, wmask, vmask, hmask, own, flip):
    lane = lax.broadcasted_iota(jnp.int32, (1, T), 1) // 16
    f = jnp.zeros((T, T), F32)
    d = jnp.zeros((T, T), F32)
    sums = []
    inner = dot(flip, i2[:T]).astype(BF)
    for g in range(8):
        here = lane == g
        back = turned(rtaps[g : g + 1]).astype(BF)
        ahead = turned(taps[g : g + 1]).astype(BF)
        w = jnp.concatenate([back, back], axis=1) * wmask
        v = jnp.concatenate([ahead, ahead], axis=1) * vmask
        f = jnp.where(here, dot(w, u2), f)
        d = jnp.where(here, dot(v, i2), d)
        mine = jnp.where(here, inner, jnp.zeros((), BF))
        pairs = dot(mine, u2, ((1,), (1,)))
        pairs = jnp.where(own, pairs[:, T:], pairs[:, :T]) * hmask
        lags = pltpu.roll(pairs, 1, 1, stride=1, stride_axis=0)
        sums.append(jnp.sum(lags, axis=0, keepdims=True))
    return f, d, jnp.concatenate(sums, axis=0)


def conv_kernel(
    q_ref, u_ref, grad_ref, inner_ref, earlier_ref, later_ref, taps_ref, rtaps_ref, gain_ref,
    wmask_ref, vmask_ref, hmask_ref, off_ref, old_ref, out_ref, send_ref, lag_ref, skip_ref,
    dq_sc, du_sc, sc,
):
    wmask = wmask_ref[...]
    vmask = vmask_ref[...]
    hmask = hmask_ref[...]
    mirrored = lax.broadcasted_iota(jnp.int32, (T, T), 0) + lax.broadcasted_iota(jnp.int32, (T, T), 1)
    own = mirrored <= T - 1
    flip = (mirrored == T - 1).astype(BF)

    def step(n, carry):
        at = pl.ds(pl.multiple_of(n * T, T), T)
        rows = pl.ds(pl.multiple_of(n * 8, 8), 8)
        u = u_ref[:, at]
        u2 = jnp.concatenate([earlier_ref[:, at], u], axis=0)
        i2 = jnp.concatenate([inner_ref[:, at], later_ref[:, at]], axis=0)
        f, d, lags = conv_block(u2, i2, taps_ref[rows], rtaps_ref[rows], wmask, vmask, hmask, own, flip)
        lag_ref[rows, :] = lags
        gain = gain_ref[:, at]
        uf = u.astype(F32)
        qf = q_ref[:, at].astype(F32)
        gf = grad_ref[:, at].astype(F32)
        inner = gf * qf
        gated = f + gain * uf
        out_ref[:, at] = (qf * gated).astype(BF)
        dq_sc[:, at] = (gf * gated).astype(BF)
        du_sc[:, at] = (d + gain * inner).astype(BF)
        skip_ref[:, at] = jnp.sum(inner * uf, axis=0, keepdims=True)
        return carry

    lax.fori_loop(0, STEP, step, 0)
    fetch = (lax.broadcasted_iota(jnp.int32, (T, T), 1) == off_ref[...]).astype(BF)
    for r in range(STEP):
        both = jnp.concatenate([dq_sc[:, lanes(r)], du_sc[:, lanes(r)]], axis=1)
        back = dot(fetch, both)
        sc[:, 0, r, :] = back[:, :T]
        sc[:, 1, r, :] = back[:, T:]
    send_ref[...] = sc[...].astype(BF)


def conv(q, u, grad, inner, earlier, later, taps, rtaps, gain, masks, off_col, out, first):
    blocks = q.shape[1] // T
    base = first // STEP
    wide = pl.BlockSpec((T, STEP * T), lambda i: (0, i))
    there = pl.BlockSpec((T, STEP * T), lambda i: (0, base + i))
    groups = pl.BlockSpec((8 * STEP, T), lambda i: (base + i, 0))
    row = pl.BlockSpec((1, STEP * T), lambda i: (0, base + i))
    whole = lambda a: pl.BlockSpec(a.shape, lambda i: (0, 0))
    alias = {} if out is None else {13: 0}
    full = jax.ShapeDtypeStruct(grad.shape, BF)
    if out is None:
        out = jnp.zeros((8, T), BF)
    return pl.pallas_call(
        conv_kernel,
        grid=(blocks // STEP,),
        in_specs=[wide, wide, there, wide, wide, wide, groups, groups, row]
        + [whole(m) for m in masks]
        + [whole(off_col), pl.BlockSpec(memory_space=pl.ANY)],
        out_specs=[
            there,
            pl.BlockSpec((T, 2, STEP, T), lambda i: (0, 0, i, 0)),
            pl.BlockSpec((8 * STEP, T), lambda i: (i, 0)),
            pl.BlockSpec((1, STEP * T), lambda i: (0, i)),
        ],
        out_shape=[
            full,
            jax.ShapeDtypeStruct((T, 2, blocks, T), BF),
            jax.ShapeDtypeStruct((8 * blocks, T), F32),
            jax.ShapeDtypeStruct((1, blocks * T), F32),
        ],
        scratch_shapes=[
            pltpu.VMEM((T, STEP * T), BF),
            pltpu.VMEM((T, STEP * T), BF),
            pltpu.VMEM((T, 2, STEP, T), F32),
        ],
        input_output_aliases=alias,
        compiler_params=pltpu.CompilerParams(vmem_limit_bytes=48 * 2**20),
        name="conv",
    )(q, u, grad, inner, earlier, later, taps, rtaps, gain, *masks, off_col, out)


def final_kernel(got_ref, k_ref, v_ref, *rest):
    q_ref, kg_ref, vg_ref, sc = rest[-4:]
    sc[...] = got_ref[...].astype(F32)
    for r in range(STEP):
        q_ref[:, lanes(r)] = sc[:, 0, r, :].astype(BF)
        du = sc[:, 1, r, :]
        kg_ref[:, lanes(r)] = (du * v_ref[:, lanes(r)].astype(F32)).astype(BF)
        vg_ref[:, lanes(r)] = (du * k_ref[:, lanes(r)].astype(F32)).astype(BF)


def final(got, k, v, outs, first):
    blocks = got.shape[2]
    there = pl.BlockSpec((T, STEP * T), lambda i: (0, first // STEP + i))
    outs = outs or []
    return pl.pallas_call(
        final_kernel,
        grid=(blocks // STEP,),
        in_specs=[pl.BlockSpec((T, 2, STEP, T), lambda i: (0, 0, i, 0)), there, there]
        + [pl.BlockSpec(memory_space=pl.ANY)] * len(outs),
        out_specs=[there] * 3,
        out_shape=[jax.ShapeDtypeStruct(k.shape, BF)] * 3,
        scratch_shapes=[pltpu.VMEM((T, 2, STEP, T), F32)],
        input_output_aliases={3 + i: i for i in range(len(outs))},
        compiler_params=pltpu.CompilerParams(vmem_limit_bytes=40 * 2**20),
        name="final",
    )(got, k, v, *outs)


def exchange(x):
    return lax.all_to_all(x, ("dp", "ctx"), split_axis=0, concat_axis=0, tiled=True)


def masks_of(genome_len, ctx_size):
    ends = jnp.cumsum(genome_len.reshape(-1))
    start = lax.axis_index("ctx") * T
    position = start - T + jnp.arange(3 * T, dtype=jnp.int32)
    inside = (position >= 0) & (position < T * ctx_size)
    segment = jnp.sum((position[:, None] >= ends[None, :]).astype(jnp.int32), axis=1)
    segment = jnp.where(inside, segment, -1)
    before, own, after = segment[:T], segment[T : 2 * T], segment[2 * T :]
    i = jnp.arange(T, dtype=jnp.int32)[:, None]
    m = jnp.arange(T, dtype=jnp.int32)[None, :]
    same = own[:, None] == own[None, :]
    same_before = own[:, None] == before[None, :]
    same_after = own[:, None] == after[None, :]
    w_own = (m <= i) & same
    w_before = (m > i) & same_before
    wmask = jnp.concatenate([w_before, w_own], axis=1).astype(BF)
    vmask = jnp.concatenate([(m >= i) & same, (m < i) & same_after], axis=1).astype(BF)
    return wmask, vmask, (w_own | w_before).astype(F32)[::-1]


def body(q_rows, k_rows, v_rows, out_grad, filters, skip_gain, genome_len, plan_offset):
    chans = q_rows.shape[1]
    members = lax.axis_size("dp") * lax.axis_size("ctx")
    groups = filters.shape[0]
    ctx_size = lax.axis_size("ctx")
    total = members * q_rows.shape[0]
    blocks = chans // T // NC
    off_row = plan_offset.reshape(1, T)
    off_col = plan_offset.reshape(T, 1)
    masks = masks_of(genome_len, ctx_size)
    taps = filters.astype(BF).astype(F32)
    rtaps = jnp.concatenate([taps[:, :1], taps[:, :0:-1]], axis=1)
    gain = skip_gain.reshape(1, chans)
    firsts = [c * blocks for c in range(NC)]
    sent = [prep(q_rows, k_rows, v_rows, first, blocks) for first in firsts]
    got = [exchange(s) for s in sent]
    up = [(i, i + 1) for i in range(ctx_size - 1)]
    down = [(i + 1, i) for i in range(ctx_size - 1)]
    out = None
    returned, lags, skips = [], [], []
    for first, g in zip(firsts, got):
        q, u, inner = plan(g, out_grad, off_row, first)
        earlier = lax.ppermute(u, "ctx", up)
        later = lax.ppermute(inner, "ctx", down)
        out, send, lag, skip = conv(
            q, u, out_grad, inner, earlier, later, taps, rtaps, gain, masks, off_col, out, first
        )
        returned.append(exchange(send))
        lags.append(lag)
        skips.append(skip)
    lag = jnp.concatenate(lags, axis=0).reshape(members, groups // members, T)
    skip = jnp.concatenate(skips, axis=1).reshape(members, 1, chans // members)
    skip = jnp.pad(skip, ((0, 0), (0, 0), (0, T - chans // members)))
    terms = exchange(jnp.pad(jnp.concatenate([lag, skip], axis=1), ((0, 0), (0, 3), (0, 0))))
    sums = jnp.sum(terms, axis=0)
    lag_sum = sums[: groups // members]
    lag_sum = jnp.concatenate([lag_sum[:, :1], lag_sum[:, :0:-1]], axis=1)
    filter_grad = lag_sum / math.sqrt(total * (chans // groups))
    skip_grad = sums[groups // members, : chans // members] / math.sqrt(total)
    outs = None
    for first, r in zip(firsts, returned):
        outs = final(r, k_rows, v_rows, outs, first)
    return (out, *outs, filter_grad, skip_grad)


def solution(mesh):
    rows = P(("dp", "ctx"), None)
    return jax.shard_map(
        body,
        mesh=mesh,
        in_specs=(rows, rows, rows, rows, P(), P(), P("dp", None), P(None, ("dp", "ctx"), None)),
        out_specs=(rows, rows, rows, rows, rows, P(("dp", "ctx"))),
        check_vma=False,
    )
```

time: 925 us -> 270 us (0.29); the launches traced: 911 us -> 270 us
  local copies, waits for them, and re-layouts: 503 us -> 17.2 us
  matrix products: 97.6 us -> 0 us
  Pallas kernels: 0 us -> 94.6 us
  other arithmetic: 91.2 us -> 2.13 us
  waiting for transfers between devices: 104 us -> 62.4 us
  between operations: 14.9 us -> 0.86 us
    reshape x29 -> x2, local copies, waits for them, and re-layouts: 218 us -> 0.19 us  [the longest x1 0.11 us: body(): off_col = plan_offset.reshape(T, 1)]
    another operation x12 -> x0, local copies, waits for them, and re-layouts: 119 us -> none  [the longest x8 69.4 us: toeplitz(): tiled = jnp.tile(edge, (1, tap_count))]
    dot_general x16 -> x0, matrix products: 97.6 us -> none  [the longest x4 31 us: body(): jnp.einsum('gim,sbmgc->sbigc', matrix, pieces, preferred_element_type=jnp...]
    pallas_call x0 -> x8, Pallas kernels: none -> 94.6 us  [the longest x2 59.4 us: conv(): pl.pallas_call(conv_kernel, grid=(blocks // STEP,), in_specs=[wide, wide,...]
    unnamed x2 -> x0, waiting for transfers between devices: 68.2 us -> none
    unnamed x1 -> x0, blocking collectives: 67.7 us -> none
    all_to_all x0 -> x2, blocking collectives: none -> 59.9 us  [exchange(): lax.all_to_all(x, ('dp', 'ctx'), split_axis=0, concat_axis=0, tiled=True)]
    unnamed x46 -> x38, local copies, waits for them, and re-layouts: 73.3 us -> 16.3 us
  transfers between devices with their start and end apart: 7 -> 7, of which waited for: 3 -> 5; matrix products, arithmetic and copies ran while one was open for 52% -> 1% of each run, Pallas kernels for 0% -> 19%
where the time goes in v1:
time: 270 us
  Pallas kernels  94.6 us (35%)
  waiting for transfers between devices  62.4 us (23%)
  blocking collectives  59.9 us (22%)
  starting transfers between devices  32.4 us (12%)
  local copies, waits for them, and re-layouts  17.2 us (6%)
    all_to_all x2, blocking collectives, exchange(): lax.all_to_all(x, ('dp', 'ctx'), split_axis=0, concat_axis=0, tiled=True)  59.9 us
    pallas_call x2, Pallas kernels, conv(): pl.pallas_call(conv_kernel, grid=(blocks // STEP,), in_specs=[wide, wide,...  59.4 us
    all_to_all x3, waiting for transfers between devices, exchange(): lax.all_to_all(x, ('dp', 'ctx'), split_axis=0, concat_axis=0, tiled=True)  58.6 us
    all_to_all x3, starting transfers between devices, exchange(): lax.all_to_all(x, ('dp', 'ctx'), split_axis=0, concat_axis=0, tiled=True)  21.9 us
    pallas_call x2, Pallas kernels, final(): pl.pallas_call(final_kernel, grid=(blocks // STEP,), in_specs=[pl.BlockSp...  17 us
    unnamed x38, local copies, waits for them, and re-layouts  16.3 us
    pallas_call x2, Pallas kernels, plan(): pl.pallas_call(plan_kernel, grid=(blocks // STEP,), in_specs=[pl.BlockSpe...  11.2 us
    ppermute x2, starting transfers between devices, body(): earlier = lax.ppermute(u, 'ctx', up)  7.62 us
  transfers between devices with their start and end apart: 7, of which 5 were waited for; matrix products, arithmetic and copies ran while one was open for 1% of the time, Pallas kernels for 19%

profile of v1, /device:TPU:1, one launch (start us, length us, event | category | flops | bytes accessed | tf_op | source)
XLA Modules:
  0.0 269.6 jit_solution(17911336590144227988)
XLA Ops:
  2.2 1.6 copy-done.4
  3.8 1.6 copy-done.11
  5.4 3.6 %prep.3 = bf16[128,2,32,128]{3,2,1,0:T(8,128)(2,1)S(1)} custom-call(bf16[128,8192]{1,0:T(8,128)(2,1)S(1)} %copy-done.11, bf16[128,8192]{1,0:T(8,128)(2,1)S(1)} %copy-done.1, bf16[128,8192]{1,0:T(8,128)(2,1)S(1)} %copy-done.4), custom_call_target="tpu_custom_call" | custom-call | tf_op jit(solution)/shard_map/prep/pallas_call | solution.py:37
  10.3 12.0 %all-to-all-start.1 = ((bf16[128,2,32,128]{3,2,1,0:T(8,128)(2,1)}), bf16[128,2,32,128]{3,2,1,0:T(8,128)(2,1)}, u32[]{:S(2)}, u32[]{:S(2)}) async-start(bf16[128,2,32,128]{3,2,1,0:T(8,128)(2,1)} %copy-done.10), calls=%async_computation.1 | async-start | bytes 4194304 | tf_op jit(solution)/shard_map/all_to_all | solution.py:221
  25.5 3.6 %prep.2 = bf16[128,2,32,128]{3,2,1,0:T(8,128)(2,1)S(1)} custom-call(bf16[128,8192]{1,0:T(8,128)(2,1)S(1)} %copy-done.12, bf16[128,8192]{1,0:T(8,128)(2,1)S(1)} %copy-done.2, bf16[128,8192]{1,0:T(8,128)(2,1)S(1)} %copy-done.5), custom_call_target="tpu_custom_call" | custom-call | tf_op jit(solution)/shard_map/prep/pallas_call | solution.py:37
  30.4 22.4 %all-to-all-done.1.got_ref = bf16[128,2,32,128]{3,2,1,0:T(8,128)(2,1)} async-done(((bf16[128,2,32,128]{3,2,1,0:T(8,128)(2,1)}), bf16[128,2,32,128]{3,2,1,0:T(8,128)(2,1)}, u32[]{:S(2)}, u32[]{:S(2)}) %all-to-all-start.1) | async-done | bytes 2097184 | tf_op jit(solution)/shard_map/all_to_all | solution.py:221
  52.7 4.9 %all-to-all-start = ((bf16[128,2,32,128]{3,2,1,0:T(8,128)(2,1)}), bf16[128,2,32,128]{3,2,1,0:T(8,128)(2,1)}, u32[]{:S(2)}, u32[]{:S(2)}) async-start(bf16[128,2,32,128]{3,2,1,0:T(8,128)(2,1)} %copy-done.9), calls=%async_computation | async-start | bytes 4194304 | tf_op jit(solution)/shard_map/all_to_all | solution.py:221
  58.1 5.6 %plan.3 = (bf16[128,4096]{1,0:T(8,128)(2,1)S(1)}, bf16[128,4096]{1,0:T(8,128)(2,1)}, bf16[128,4096]{1,0:T(8,128)(2,1)}) custom-call(bf16[128,2,32,128]{3,2,1,0:T(8,128)(2,1)} %all-to-all-done.1.got_ref, bf16[128,8192]{1,0:T(8,128)(2,1)S(1)} %copy-done, s32[1,128]{1,0:T(1,128)S(1)} %bitcast.14), custom_call_target="tpu_custom_call" | custom-call | tf_op jit(solution)/shard_map/plan/pallas_call | solution.py:66
  64.7 4.3 %collective-permute-start.2 = (bf16[128,4096]{1,0:T(8,128)(2,1)}, bf16[128,4096]{1,0:T(8,128)(2,1)}, u32[]{:S(2)}, u32[]{:S(2)}) collective-permute-start(bf16[128,4096]{1,0:T(8,128)(2,1)} %get-tuple-element.30.u_ref), channel_id=1, source_target_pairs={{0,1},{1,2},{2,3},{4,5},{5,6},{6,7},{8,9},{9,10},{10,11},{12,13},{... | collective-permute-start | bytes 3145736 | tf_op jit(solution)/shard_map/ppermute | solution.py:266
  70.4 18.3 %all-to-all-done.got_ref = bf16[128,2,32,128]{3,2,1,0:T(8,128)(2,1)} async-done(((bf16[128,2,32,128]{3,2,1,0:T(8,128)(2,1)}), bf16[128,2,32,128]{3,2,1,0:T(8,128)(2,1)}, u32[]{:S(2)}, u32[]{:S(2)}) %all-to-all-start) | async-done | bytes 2097184 | tf_op jit(solution)/shard_map/all_to_all | solution.py:221
  88.7 5.5 %plan.2 = (bf16[128,4096]{1,0:T(8,128)(2,1)S(1)}, bf16[128,4096]{1,0:T(8,128)(2,1)}, bf16[128,4096]{1,0:T(8,128)(2,1)}) custom-call(bf16[128,2,32,128]{3,2,1,0:T(8,128)(2,1)} %all-to-all-done.got_ref, bf16[128,8192]{1,0:T(8,128)(2,1)S(1)} %copy-done, s32[1,128]{1,0:T(1,128)S(1)} %bitcast.15), custom_call_target="tpu_custom_call" | custom-call | tf_op jit(solution)/shard_map/plan/pallas_call | solution.py:66
  94.2 3.3 %collective-permute-start = (bf16[128,4096]{1,0:T(8,128)(2,1)}, bf16[128,4096]{1,0:T(8,128)(2,1)}, u32[]{:S(2)}, u32[]{:S(2)}) collective-permute-start(bf16[128,4096]{1,0:T(8,128)(2,1)} %get-tuple-element.27.u_ref), channel_id=1, source_target_pairs={{0,1},{1,2},{2,3},{4,5},{5,6},{6,7},{8,9},{9,10},{10,11},{12,13},{... | collective-permute-start | bytes 3145736 | tf_op jit(solution)/shard_map/ppermute | solution.py:266
  100.8 2.9 %collective-permute-done.3.later_ref = bf16[128,4096]{1,0:T(8,128)(2,1)} collective-permute-done((bf16[128,4096]{1,0:T(8,128)(2,1)}, bf16[128,4096]{1,0:T(8,128)(2,1)}, u32[]{:S(2)}, u32[]{:S(2)}) %collective-permute-start.3) | collective-permute-done | bytes 1048608 | tf_op jit(solution)/shard_map/ppermute | solution.py:267
  103.7 29.7 %conv.2 = (bf16[128,8192]{1,0:T(8,128)(2,1)}, bf16[128,2,32,128]{3,2,1,0:T(8,128)(2,1)}, f32[256,128]{1,0:T(8,128)S(1)}, f32[1,4096]{1,0:T(1,128)S(1)}) custom-call(bf16[128,4096]{1,0:T(8,128)(2,1)S(1)} %copy-done.14, bf16[128,4096]{1,0:T(8,128)(2,1)} %get-tuple-element.30.u_ref, bf16[128,8192]{1,0:T(8,128)(2,1)} %grad_ref.7, ...), custom_call_target="tpu_custom_call" | custom-call | tf_op jit(solution)/shard_map/conv/pallas_call | solution.py:163
  133.4 29.7 %conv.3 = (bf16[128,8192]{1,0:T(8,128)(2,1)}, bf16[128,2,32,128]{3,2,1,0:T(8,128)(2,1)}, f32[256,128]{1,0:T(8,128)S(1)}, f32[1,4096]{1,0:T(1,128)S(1)}) custom-call(bf16[128,4096]{1,0:T(8,128)(2,1)S(1)} %get-tuple-element.26.q_ref, bf16[128,4096]{1,0:T(8,128)(2,1)} %get-tuple-element.27.u_ref, ...), custom_call_target="tpu_custom_call", output_to_operand_aliasing={{0}: (13, {})} | custom-call | tf_op jit(solution)/shard_map/conv/pallas_call | solution.py:163
  163.5 24.2 %all_to_all.25 = f32[128,8,128]{2,1,0:T(8,128)S(1)} all-to-all(f32[128,8,128]{2,1,0:T(8,128)S(1)} %select_maximum_fusion), channel_id=1, replica_groups=mesh['dp'=32,'ctx'=4] {'dp','ctx'}, dimensions={0} | all-to-all | bytes 1048576 | tf_op jit(solution)/shard_map/all_to_all | solution.py:221
  187.6 35.7 %all_to_all.26.got_ref = bf16[128,2,32,128]{3,2,1,0:T(8,128)(2,1)} all-to-all(bf16[128,2,32,128]{3,2,1,0:T(8,128)(2,1)} %get-tuple-element.35), channel_id=1, replica_groups=mesh['dp'=32,'ctx'=4] {'dp','ctx'}, dimensions={0} | all-to-all | bytes 4194304 | tf_op jit(solution)/shard_map/all_to_all | solution.py:221
  223.4 5.1 %all-to-all-start.2 = ((bf16[128,2,32,128]{3,2,1,0:T(8,128)(2,1)}), bf16[128,2,32,128]{3,2,1,0:T(8,128)(2,1)}, u32[]{:S(2)}, u32[]{:S(2)}) async-start(bf16[128,2,32,128]{3,2,1,0:T(8,128)(2,1)} %get-tuple-element.34), calls=%async_computation.2 | async-start | bytes 4194304 | tf_op jit(solution)/shard_map/all_to_all | solution.py:221
  229.9 1.6 copy-done.6
  231.5 1.6 copy-done.8
  233.1 8.0 %final.2 = (bf16[128,8192]{1,0:T(8,128)(2,1)}, bf16[128,8192]{1,0:T(8,128)(2,1)}, bf16[128,8192]{1,0:T(8,128)(2,1)}) custom-call(bf16[128,2,32,128]{3,2,1,0:T(8,128)(2,1)S(1)} %copy-done.8, bf16[128,8192]{1,0:T(8,128)(2,1)S(1)} %copy-done.3, bf16[128,8192]{1,0:T(8,128)(2,1)S(1)} %copy-done.6), custom_call_target="tpu_custom_call" | custom-call | tf_op jit(solution)/shard_map/final/pallas_call | solution.py:206
  241.1 17.9 %all-to-all-done.2.got_ref = bf16[128,2,32,128]{3,2,1,0:T(8,128)(2,1)} async-done(((bf16[128,2,32,128]{3,2,1,0:T(8,128)(2,1)}), bf16[128,2,32,128]{3,2,1,0:T(8,128)(2,1)}, u32[]{:S(2)}, u32[]{:S(2)}) %all-to-all-start.2) | async-done | bytes 2097184 | tf_op jit(solution)/shard_map/all_to_all | solution.py:221
  259.0 1.6 copy-done.7
  260.6 9.0 %final.3 = (bf16[128,8192]{1,0:T(8,128)(2,1)}, bf16[128,8192]{1,0:T(8,128)(2,1)}, bf16[128,8192]{1,0:T(8,128)(2,1)}) custom-call(bf16[128,2,32,128]{3,2,1,0:T(8,128)(2,1)} %all-to-all-done.2.got_ref, bf16[128,8192]{1,0:T(8,128)(2,1)S(1)} %copy-done.3, bf16[128,8192]{1,0:T(8,128)(2,1)S(1)} %copy-done.7, ...), custom_call_target="tpu_custom_call", output_to_operand_aliasing={{0}: (3, {}), {1}: (4, {}), {2}: (5, {})} | custom-call | tf_op jit(solution)/shard_map/final/pallas_call | solution.py:206
  (63 shorter events, 15.2 us)
Async XLA Ops:
  0.6 1.6 copy-start.1
  2.2 1.6 copy-start.4
  3.8 1.6 copy-start.11
  9.0 1.3 copy-start.10
  10.3 12.0 %copy-start.2 = (bf16[128,8192]{1,0:T(8,128)(2,1)S(1)}, bf16[128,8192]{1,0:T(8,128)(2,1)}, u32[]{:S(2)}) copy-start(bf16[128,8192]{1,0:T(8,128)(2,1)} %k_ref.7) | copy-start | bytes 6291460
  10.3 42.4 %all-to-all-start.1 = ((bf16[128,2,32,128]{3,2,1,0:T(8,128)(2,1)}), bf16[128,2,32,128]{3,2,1,0:T(8,128)(2,1)}, u32[]{:S(2)}, u32[]{:S(2)}) async-start(bf16[128,2,32,128]{3,2,1,0:T(8,128)(2,1)} %copy-done.10), calls=%async_computation.1 | async-start | bytes 4194304 | tf_op jit(solution)/shard_map/all_to_all | solution.py:221
  22.3 1.6 copy-start.5
  23.9 1.6 copy-start.12
  30.4 27.3 %copy-start.16 = (s32[128,1,1]{0,2,1:T(1,128)S(1)}, s32[128,1,1]{0,2,1:T(1,128)}, u32[]{:S(2)}) copy-start(s32[128,1,1]{0,2,1:T(1,128)} %param.15) | copy-start | bytes 1540
  30.4 27.4 %copy-start.18 = (s32[1,3]{1,0:T(1,128)S(1)}, s32[1,3]{1,0:T(1,128)}, u32[]{:S(2)}) copy-start(s32[1,3]{1,0:T(1,128)} %param.14) | copy-start | bytes 40
  30.4 27.7 %copy-start = (bf16[128,8192]{1,0:T(8,128)(2,1)S(1)}, bf16[128,8192]{1,0:T(8,128)(2,1)}, u32[]{:S(2)}) copy-start(bf16[128,8192]{1,0:T(8,128)(2,1)} %grad_ref.7) | copy-start | bytes 6291460
  52.7 35.9 %all-to-all-start = ((bf16[128,2,32,128]{3,2,1,0:T(8,128)(2,1)}), bf16[128,2,32,128]{3,2,1,0:T(8,128)(2,1)}, u32[]{:S(2)}, u32[]{:S(2)}) async-start(bf16[128,2,32,128]{3,2,1,0:T(8,128)(2,1)} %copy-done.9), calls=%async_computation | async-start | bytes 4194304 | tf_op jit(solution)/shard_map/all_to_all | solution.py:221
  64.7 36.1 %collective-permute-start.2 = (bf16[128,4096]{1,0:T(8,128)(2,1)}, bf16[128,4096]{1,0:T(8,128)(2,1)}, u32[]{:S(2)}, u32[]{:S(2)}) collective-permute-start(bf16[128,4096]{1,0:T(8,128)(2,1)} %get-tuple-element.30.u_ref), channel_id=1, source_target_pairs={{0,1},{1,2},{2,3},{4,5},{5,6},{6,7},{8,9},{9,10},{10,11},{12,13},{... | collective-permute-start | bytes 3145736 | tf_op jit(solution)/shard_map/ppermute | solution.py:266
  69.0 30.2 %copy-start.17 = (f32[512,128]{1,0:T(8,128)S(1)}, f32[512,128]{1,0:T(8,128)}, u32[]{:S(2)}) copy-start(f32[512,128]{1,0:T(8,128)} %param.12) | copy-start | bytes 786436
  69.0 34.8 %collective-permute-start.3 = (bf16[128,4096]{1,0:T(8,128)(2,1)}, bf16[128,4096]{1,0:T(8,128)(2,1)}, u32[]{:S(2)}, u32[]{:S(2)}) collective-permute-start(bf16[128,4096]{1,0:T(8,128)(2,1)} %get-tuple-element.31.inner_ref), channel_id=1, source_target_pairs={{1,0},{2,1},{3,2},{5,4},{6,5},{7,6},{9,8},{10,9},{11,10},{13,12},{... | collective-permute-start | bytes 3145736 | tf_op jit(solution)/shard_map/ppermute | solution.py:267
  94.2 9.5 %copy-start.14 = (bf16[128,4096]{1,0:T(8,128)(2,1)S(1)}, bf16[128,4096]{1,0:T(8,128)(2,1)}, u32[]{:S(2)}) copy-start(bf16[128,4096]{1,0:T(8,128)(2,1)} %copy-done.13) | copy-start | bytes 3145732
  94.2 9.5 %copy-start.15 = (f32[8192]{0:T(1024)S(1)}, f32[8192]{0:T(1024)}, u32[]{:S(2)}) copy-start(f32[8192]{0:T(1024)} %param.13) | copy-start | bytes 98308
  94.2 39.2 %collective-permute-start = (bf16[128,4096]{1,0:T(8,128)(2,1)}, bf16[128,4096]{1,0:T(8,128)(2,1)}, u32[]{:S(2)}, u32[]{:S(2)}) collective-permute-start(bf16[128,4096]{1,0:T(8,128)(2,1)} %get-tuple-element.27.u_ref), channel_id=1, source_target_pairs={{0,1},{1,2},{2,3},{4,5},{5,6},{6,7},{8,9},{9,10},{10,11},{12,13},{... | collective-permute-start | bytes 3145736 | tf_op jit(solution)/shard_map/ppermute | solution.py:266
  97.5 35.9 %collective-permute-start.1 = (bf16[128,4096]{1,0:T(8,128)(2,1)}, bf16[128,4096]{1,0:T(8,128)(2,1)}, u32[]{:S(2)}, u32[]{:S(2)}) collective-permute-start(bf16[128,4096]{1,0:T(8,128)(2,1)} %get-tuple-element.28.inner_ref), channel_id=1, source_target_pairs={{1,0},{2,1},{3,2},{5,4},{6,5},{7,6},{9,8},{10,9},{11,10},{13,12},{... | collective-permute-start | bytes 3145736 | tf_op jit(solution)/shard_map/ppermute | solution.py:267
  223.4 6.6 %copy-start.3 = (bf16[128,8192]{1,0:T(8,128)(2,1)S(1)}, bf16[128,8192]{1,0:T(8,128)(2,1)}, u32[]{:S(2)}) copy-start(bf16[128,8192]{1,0:T(8,128)(2,1)} %k_ref.7) | copy-start | bytes 6291460
  223.4 35.6 %all-to-all-start.2 = ((bf16[128,2,32,128]{3,2,1,0:T(8,128)(2,1)}), bf16[128,2,32,128]{3,2,1,0:T(8,128)(2,1)}, u32[]{:S(2)}, u32[]{:S(2)}) async-start(bf16[128,2,32,128]{3,2,1,0:T(8,128)(2,1)} %get-tuple-element.34), calls=%async_computation.2 | async-start | bytes 4194304 | tf_op jit(solution)/shard_map/all_to_all | solution.py:221
  229.9 1.6 copy-start.6
  231.5 1.6 copy-start.8
  259.0 1.6 copy-start.7
  (2 other events, 2.3 us)
